TPU v7x, 512 devices: a whole 4x4x16 slice. The times are simulated.
512 devices in a mesh: grp: 4 (over z_hi, core), seq: 128 (over x, y, z_lo).
Axes of the slice: x: 4, y: 4, z: 16 (z_hi: 2, z_lo: 8; z = z_hi * 8 + z_lo), core: 2. Of those that a mesh axis runs over, the one named last changes fastest.
Arguments:
- cand_queries: bfloat16 [4096, 128, 128], P(('grp', 'seq')), may hold values from -256 to 256
- candidate_keys: bfloat16 [512, 128, 128], P(('grp', 'seq')), may hold values from -6 to 6
- candidate_values: bfloat16 [512, 128, 128], P(('grp', 'seq')), may hold values from -24 to 24
- prefix_rotated_keys: bfloat16 [2048, 1024], P(('grp', 'seq')), may hold values from -6.1 to 6.1
- prefix_value_matrix: bfloat16 [2048, 1024], P(('grp', 'seq')), may hold values from -24 to 24
- lengths: int32 [64], replicated, may hold values from 32 to 128
Outputs:
- attended: bfloat16 [4096, 128, 128], P(('grp', 'seq'))
All inputs are finite; a program needn't handle non-finite values.
Results may differ from a plain program's by a relative error of at most 0.0076.
Values may be sent and summed in bfloat16 or wider, within the bound.
A program may use at most 64 MiB of HBM per device.

v0:
```python
import math
import jax
import jax.numpy as jnp
import numpy as np
from jax import lax
from jax.sharding import PartitionSpec as P

QUERY_HEADS = 64
KEY_VALUE_HEADS = 8
HEAD_WIDTH = 128
rope_base = 500000.0


def in_one_piece(arrays, axis, dim, along):
    both = jnp.concatenate(arrays, axis=along)
    filled, at, outs = (lax.all_gather(both, axis, axis=dim, tiled=True), 0, [])
    for a in arrays:
        outs.append(lax.slice_in_dim(filled, at, at + a.shape[along], axis=along))
        at += a.shape[along]
    return tuple(outs)


def rotate(vectors, positions):
    half_width = vectors.shape[-1] // 2
    exponents = jnp.arange(half_width, dtype=jnp.float32) * (2.0 / vectors.shape[-1])
    frequency = 1.0 / jnp.power(jnp.float32(rope_base), exponents)
    angles = positions.astype(jnp.float32)[:, None] * frequency[None, :]
    cosine = jnp.cos(angles)
    sine_table = jnp.sin(angles)
    lower_half = vectors[..., :half_width]
    upper_half = vectors[..., half_width:]
    return jnp.concatenate(
        [
            lower_half * cosine - upper_half * sine_table,
            upper_half * cosine + lower_half * sine_table,
        ],
        axis=-1,
    )


def pick_heads(key_row_list, value_row_list, head_table, sequence_count):
    row_total = key_row_list.shape[0]
    stacked = jnp.stack(
        [
            key_row_list.reshape(row_total, KEY_VALUE_HEADS, HEAD_WIDTH),
            value_row_list.reshape(row_total, KEY_VALUE_HEADS, HEAD_WIDTH),
        ],
        axis=2,
    )
    picked = jnp.take(stacked, head_table, axis=1)
    return picked.reshape(row_total, sequence_count, -1).transpose(1, 0, 2)


def shards(
    cand_queries,
    candidate_keys,
    candidate_values,
    prefix_rotated_keys,
    prefix_value_matrix,
    lengths,
):
    sequence_count = lax.axis_size("seq")
    grp_count = lax.axis_size("grp")
    head_rows = cand_queries.shape[0]
    cand_length = cand_queries.shape[1]
    key_value_rows = candidate_keys.shape[0]
    group_width = QUERY_HEADS // KEY_VALUE_HEADS
    key_value_heads = min(KEY_VALUE_HEADS, key_value_rows)
    prefix_here = prefix_rotated_keys.shape[0]
    prefix_total = prefix_here * sequence_count * grp_count
    score_scale = 1.0 / math.sqrt(HEAD_WIDTH)
    prefix_pick = (
        (np.arange(sequence_count)[:, None] * key_value_rows + np.arange(key_value_heads)[None, :])
        % KEY_VALUE_HEADS
    ).reshape(-1)
    copies = in_one_piece((prefix_rotated_keys, prefix_value_matrix), "grp", 0, 1)
    outgoing = pick_heads(copies[0], copies[1], prefix_pick, sequence_count)
    prefix_pair = lax.all_to_all(outgoing, "seq", split_axis=0, concat_axis=1, tiled=True)
    prefix_pair = prefix_pair.reshape(prefix_total, key_value_heads, 2, HEAD_WIDTH)
    kv_table = np.arange(key_value_rows) % key_value_heads
    prefix_key_rows = jnp.take(prefix_pair[:, :, 0], kv_table, axis=1).transpose(1, 0, 2)
    prefix_value_rows = jnp.take(prefix_pair[:, :, 1], kv_table, axis=1).transpose(1, 0, 2)
    positions = prefix_total + jnp.arange(cand_length, dtype=jnp.int32)
    new_keys = rotate(candidate_keys.astype(jnp.float32), positions).astype(jnp.bfloat16)
    rotated = rotate(cand_queries.astype(jnp.float32), positions).astype(jnp.bfloat16)
    rotated = rotated.reshape(key_value_rows, group_width * cand_length, HEAD_WIDTH)
    all_keys = jnp.concatenate([prefix_key_rows, new_keys], axis=1)
    all_values = jnp.concatenate([prefix_value_rows, candidate_values], axis=1)
    key_count = prefix_total + cand_length
    block_rows = math.gcd(key_count, 512)
    block_count = key_count // block_rows
    row_total = group_width * cand_length
    row_token = jnp.arange(row_total, dtype=jnp.int32) % cand_length
    starts = jnp.arange(block_count, dtype=jnp.int32) * block_rows

    def attend(carry, block):
        maxima, totals, weighted = carry
        block_keys, block_values, first_row = block
        scores = (
            jnp.einsum("krd,knd->krn", rotated, block_keys, preferred_element_type=jnp.float32)
            * score_scale
        )
        cand_offset = first_row + jnp.arange(block_rows, dtype=jnp.int32) - prefix_total
        scores = jnp.where((cand_offset[None, :] <= row_token[:, None])[None], scores, -jnp.inf)
        highest = jnp.maximum(maxima, jnp.max(scores, axis=-1))
        decline = jnp.exp(maxima - highest)
        exponent = jnp.exp(scores - highest[..., None])
        totals = totals * decline + jnp.sum(exponent, axis=-1)
        weighted = weighted * decline[..., None] + jnp.einsum(
            "krn,knd->krd",
            exponent.astype(jnp.bfloat16),
            block_values,
            preferred_element_type=jnp.float32,
        )
        return ((highest, totals, weighted), None)

    start_state = (
        jnp.full((key_value_rows, row_total), -1e30, jnp.float32),
        jnp.zeros((key_value_rows, row_total), jnp.float32),
        jnp.zeros((key_value_rows, row_total, HEAD_WIDTH), jnp.float32),
    )
    key_blocks = all_keys.reshape(key_value_rows, block_count, block_rows, HEAD_WIDTH).transpose(
        1, 0, 2, 3
    )
    value_blocks = all_values.reshape(
        key_value_rows, block_count, block_rows, HEAD_WIDTH
    ).transpose(1, 0, 2, 3)
    final_state, unused = lax.scan(attend, start_state, (key_blocks, value_blocks, starts))
    maxima, totals, weighted = final_state
    attended = (weighted / totals[..., None]).reshape(head_rows, cand_length, HEAD_WIDTH)
    device_place = lax.axis_index("grp") * sequence_count + lax.axis_index("seq")
    cand_of_row = (device_place * head_rows + jnp.arange(head_rows, dtype=jnp.int32)) // QUERY_HEADS
    cand_slots = jnp.arange(lengths.shape[0], dtype=jnp.int32)
    cand_limit = jnp.sum(
        jnp.where(cand_of_row[:, None] == cand_slots[None, :], lengths[None, :], 0), axis=1
    )
    visible = jnp.arange(cand_length, dtype=jnp.int32)[None, :] < cand_limit[:, None]
    return jnp.where(visible[:, :, None], attended, jnp.float32(0.0)).astype(jnp.bfloat16)


def solution(mesh):
    return jax.shard_map(
        shards,
        mesh=mesh,
        in_specs=(
            P(("grp", "seq"), None, None),
            P(("grp", "seq"), None, None),
            P(("grp", "seq"), None, None),
            P(("grp", "seq"), None),
            P(("grp", "seq"), None),
            P(),
        ),
        out_specs=P(("grp", "seq"), None, None),
        check_vma=False,
    )
```

profile of v0, /device:TPU:1, one launch (start us, length us, event | category | flops | bytes accessed | tf_op | source)
XLA Modules:
  0.0 135.4 jit_solution(17232865180039130087)
XLA Ops:
  0.0 0.7 maximum_bitcast_fusion
  0.7 20.7 %all-gather = bf16[4,4,2048]{2,1,0:T(4,128)(2,1)S(1)} all-gather(bf16[1,4,2048]{2,1,0:T(4,128)(2,1)S(1)} %maximum_bitcast_fusion), channel_id=1, replica_groups=mesh['grp'=4,'seq'=128] {'grp'}, dimensions={0}, use_global_device_ids=true | all-gather | bytes 81920 | tf_op jit(solution)/shard_map/all_gather | solution.py:16
  21.5 0.7 pad_clamp_fusion
  22.2 0.8 gather_fusion
  22.9 1.1 copy.33
  24.0 1.7 %copy.34 = bf16[128,16,256]{2,1,0:T(8,128)(2,1)} copy(bf16[128,16,256]{0,2,1:T(8,128)(2,1)S(1)} %bitcast.75) | data formatting | bytes 2097152 | tf_op jit(solution)/shard_map/transpose | solution.py:51
  25.7 14.3 %all-to-all-start = ((bf16[128,16,256]{2,1,0:T(8,128)(2,1)}), bf16[128,16,256]{2,1,0:T(8,128)(2,1)S(1)}, u32[]{:S(2)}, u32[]{:S(2)}) async-start(bf16[128,16,256]{2,1,0:T(8,128)(2,1)} %copy.34), calls=%async_computation | async-start | bytes 2097152 | tf_op jit(solution)/shard_map/all_to_all | solution.py:78
  41.7 52.1 %all-to-all-done = bf16[128,16,256]{2,1,0:T(8,128)(2,1)S(1)} async-done(((bf16[128,16,256]{2,1,0:T(8,128)(2,1)}), bf16[128,16,256]{2,1,0:T(8,128)(2,1)S(1)}, u32[]{:S(2)}, u32[]{:S(2)}) %all-to-all-start) | async-done | bytes 1048608 | tf_op jit(solution)/shard_map/all_to_all | solution.py:78
  94.1 1.5 %fusion.31 = (bf16[2048,1,1,128]{3,2,0,1:T(2,128)(2,1)S(1)}, bf16[2048,1,1,128]{3,2,0,1:T(2,128)(2,1)S(1)}) fusion(bf16[2048,1,2,128]{3,2,0,1:T(2,128)(2,1)S(1)} %reshape.324), kind=kLoop, calls=%fused_computation.69 | loop fusion | bytes 2097152 | tf_op jit(solution)/shard_map/slice | solution.py:82
  95.8 0.7 copy-done.1
  96.6 37.7 %while.17 = (s32[]{:T(128)}, f32[1,1024]{1,0:T(1,128)S(1)}, f32[1,1024]{1,0:T(1,128)S(1)}, f32[1,1024,128]{2,1,0:T(8,128)S(1)}, s32[17]{0:T(128)S(1)}, /*index=5...) while((s32[]{:T(128)}, f32[1,1024]{1,0:T(1,128)S(1)}, ...), condition=%wide.region_4.5_spmd.clone, body=%wide.region_1.4_spmd.clone.sunk | while | flops 68562176 | bytes 3024009 | solution.py:128
  96.6 0.7 dynamic_slice.38
  97.3 0.7 add_add_fusion.2
  98.8 0.7 dynamic_slice.38
  99.5 0.7 add_add_fusion.2
  101.0 0.7 dynamic_slice.38
  101.7 0.7 add_add_fusion.2
  102.8 0.4 fusion.45
  103.2 0.7 dynamic_slice.38
  103.9 0.7 add_add_fusion.2
  105.0 0.4 fusion.45
  105.5 0.7 dynamic_slice.38
  106.1 0.7 add_add_fusion.2
  107.7 0.7 dynamic_slice.38
  108.3 0.7 add_add_fusion.2
  109.9 0.7 dynamic_slice.38
  110.6 0.7 add_add_fusion.2
  112.1 0.7 dynamic_slice.38
  112.8 0.7 add_add_fusion.2
  114.3 0.7 dynamic_slice.38
  115.0 0.7 add_add_fusion.2
  116.5 0.7 dynamic_slice.38
  117.2 0.7 add_add_fusion.2
  118.7 0.7 dynamic_slice.38
  119.4 0.7 add_add_fusion.2
  121.0 0.7 dynamic_slice.38
  121.6 0.7 add_add_fusion.2
  123.2 0.7 dynamic_slice.38
  123.8 0.7 add_add_fusion.2
  125.4 0.7 dynamic_slice.38
  126.1 0.7 add_add_fusion.2
  127.6 0.7 dynamic_slice.38
  128.3 0.7 add_add_fusion.2
  129.8 0.7 dynamic_slice.38
  130.5 0.7 add_add_fusion.2
  132.0 0.7 dynamic_slice.38
  132.7 0.7 add_add_fusion.2
  134.5 0.9 select_convert_fusion
  (154 shorter events, 14.8 us)
Async XLA Ops:
  25.7 14.4 %copy-start = (bf16[8,128,128]{2,1,0:T(8,128)(2,1)S(1)}, bf16[8,128,128]{2,1,0:T(8,128)(2,1)}, u32[]{:S(2)}) copy-start(bf16[8,128,128]{2,1,0:T(8,128)(2,1)} %param.10) | copy-start | bytes 786436
  25.7 14.4 %copy-start.2 = (bf16[1,128,128]{2,1,0:T(8,128)(2,1)S(1)}, bf16[1,128,128]{2,1,0:T(8,128)(2,1)}, u32[]{:S(2)}) copy-start(bf16[1,128,128]{2,1,0:T(8,128)(2,1)} %param.11) | copy-start | bytes 98308
  25.7 68.1 %all-to-all-start = ((bf16[128,16,256]{2,1,0:T(8,128)(2,1)}), bf16[128,16,256]{2,1,0:T(8,128)(2,1)S(1)}, u32[]{:S(2)}, u32[]{:S(2)}) async-start(bf16[128,16,256]{2,1,0:T(8,128)(2,1)} %copy.34), calls=%async_computation | async-start | bytes 2097152 | tf_op jit(solution)/shard_map/all_to_all | solution.py:78
  40.1 0.7 copy-start.3
  95.8 0.8 copy-start.1
where the time goes:
time: 136 us; the launch traced here: 135 us
  waiting for transfers between devices  52.1 us (38%)
  blocking collectives  20.7 us (15%)
  other arithmetic  17.9 us (13%)
  local copies, waits for them, and re-layouts  17.9 us (13%)
  starting transfers between devices  14.3 us (11%)
  matrix products  11.1 us (8%)
    all_to_all x1, waiting for transfers between devices, shards(): lax.all_to_all(outgoing, 'seq', split_axis=0, concat_axis=1, tiled=True)  52.1 us
    all_gather x1, blocking collectives, in_one_piece(): filled, at, outs = (lax.all_gather(both, axis, axis=dim, tiled=True), 0, [])  20.7 us
    all_to_all x1, starting transfers between devices, shards(): lax.all_to_all(outgoing, 'seq', split_axis=0, concat_axis=1, tiled=True)  14.3 us
    sub x17, other arithmetic, attend(): first_row + jnp.arange(block_rows, dtype=jnp.int32) - prefix_total  11.8 us
    dynamic_slice x17, local copies, waits for them, and re-layouts, shards(): lax.scan(attend, start_state, (key_blocks, value_blocks, starts))  11.3 us
    dot_general x17, matrix products, attend(): jnp.einsum('krn,knd->krd', exponent.astype(jnp.bfloat16), block_values, p...  6.91 us
    dot_general x17, matrix products, attend(): jnp.einsum('krd,knd->krn', rotated, block_keys, preferred_element_type=jn...  4.16 us
  transfers between devices with their start and end apart: 1, of which 1 were waited for; matrix products, arithmetic and copies ran while one was open for 1% of the time, Pallas kernels for 0%

commit v1 on v0

--- a/solution.py
+++ b/solution.py
@@ -75,7 +75,14 @@
     ).reshape(-1)
     copies = in_one_piece((prefix_rotated_keys, prefix_value_matrix), "grp", 0, 1)
     outgoing = pick_heads(copies[0], copies[1], prefix_pick, sequence_count)
-    prefix_pair = lax.all_to_all(outgoing, "seq", split_axis=0, concat_axis=1, tiled=True)
+
+    def wrap_the_leaves(original, dimension_no, dim_at):
+        value_now = lax.all_to_all(
+            jnp.stack(jnp.split(original, lax.axis_size("seq"), dimension_no), 0), "seq", 0, 0
+        )
+        return jnp.concatenate(value_now, dim_at)
+
+    prefix_pair = wrap_the_leaves(outgoing, 0, 1)
     prefix_pair = prefix_pair.reshape(prefix_total, key_value_heads, 2, HEAD_WIDTH)
     kv_table = np.arange(key_value_rows) % key_value_heads
     prefix_key_rows = jnp.take(prefix_pair[:, :, 0], kv_table, axis=1).transpose(1, 0, 2)

time: 136 us -> 293 us (2.15)
  local copies, waits for them, and re-layouts: 17.9 us -> 175 us
    split x0 -> x7, local copies, waits for them, and re-layouts: none -> 83.3 us  [wrap_the_leaves(): jnp.split(original, lax.axis_size('seq'), dimension_no)]
    unnamed x14 -> x141, local copies, waits for them, and re-layouts: 1.03 us -> 76.4 us
where the time goes in v1:
time: 293 us
  local copies, waits for them, and re-layouts  175 us (60%)
  waiting for transfers between devices  52.1 us (18%)
  blocking collectives  20.7 us (7%)
  other arithmetic  17.9 us (6%)
  starting transfers between devices  14.3 us (5%)
  matrix products  11.1 us (4%)
    split x7, local copies, waits for them, and re-layouts, wrap_the_leaves(): jnp.split(original, lax.axis_size('seq'), dimension_no)  83.3 us
    unnamed x141, local copies, waits for them, and re-layouts  76.4 us
    all_to_all x1, waiting for transfers between devices, wrap_the_leaves(): lax.all_to_all(jnp.stack(jnp.split(original, lax.axis_size('seq'), dimens...  52.1 us
    all_gather x1, blocking collectives, in_one_piece(): filled, at, outs = (lax.all_gather(both, axis, axis=dim, tiled=True), 0, [])  20.7 us
    all_to_all x1, starting transfers between devices, wrap_the_leaves(): lax.all_to_all(jnp.stack(jnp.split(original, lax.axis_size('seq'), dimens...  14.3 us
    sub x17, other arithmetic, attend(): first_row + jnp.arange(block_rows, dtype=jnp.int32) - prefix_total  11.8 us
    dynamic_slice x17, local copies, waits for them, and re-layouts, shards(): lax.scan(attend, start_state, (key_blocks, value_blocks, starts))  11.3 us
    dot_general x17, matrix products, attend(): jnp.einsum('krn,knd->krd', exponent.astype(jnp.bfloat16), block_values, p...  6.91 us
  transfers between devices with their start and end apart: 1, of which 1 were waited for; matrix products, arithmetic and copies ran while one was open for 1% of the time, Pallas kernels for 0%

profile of v1, /device:TPU:1, one launch (start us, length us, event | category | flops | bytes accessed | tf_op | source)
XLA Modules:
  0.0 293.0 jit_solution(2975652573965990210)
XLA Ops:
  0.0 0.7 maximum_bitcast_fusion
  0.7 20.7 %all-gather = bf16[4,4,2048]{2,1,0:T(4,128)(2,1)S(1)} all-gather(bf16[1,4,2048]{2,1,0:T(4,128)(2,1)S(1)} %maximum_bitcast_fusion), channel_id=1, replica_groups=mesh['grp'=4,'seq'=128] {'grp'}, dimensions={0}, use_global_device_ids=true | all-gather | bytes 81920 | tf_op jit(solution)/shard_map/all_gather | solution.py:16
  22.2 0.8 gather_fusion
  22.9 1.1 copy.3646
  24.0 8.7 %slice_reduce_fusion.114 = (bf16[16,256]{1,0:T(8,128)(2,1)S(1)}, bf16[16,256]{1,0:T(8,128)(2,1)S(1)}, bf16[16,256]{1,0:T(8,128)(2,1)S(1)}, bf16[16,256]{1,0:T(8,...) fusion(bf16[128,16,256]{0,2,1:T(8,128)(2,1)S(1)} %bitcast.332), kind=kLoop, calls=%fused_computation.145 | loop fusion | bytes 229376 | tf_op jit(solution)/shard_map/split | solution.py:81
  32.8 12.4 %slice_reduce_fusion.95 = (bf16[16,256]{1,0:T(8,128)(2,1)S(1)}, bf16[16,256]{1,0:T(8,128)(2,1)S(1)}, bf16[16,256]{1,0:T(8,128)(2,1)S(1)}, bf16[16,256]{1,0:T(8,1...) fusion(bf16[128,16,256]{0,2,1:T(8,128)(2,1)S(1)} %bitcast.333), kind=kLoop, calls=%fused_computation.126 | loop fusion | bytes 311296 | tf_op jit(solution)/shard_map/split | solution.py:81
  45.1 12.4 %slice_reduce_fusion.76 = (bf16[16,256]{1,0:T(8,128)(2,1)S(1)}, bf16[16,256]{1,0:T(8,128)(2,1)S(1)}, bf16[16,256]{1,0:T(8,128)(2,1)S(1)}, bf16[16,256]{1,0:T(8,1...) fusion(bf16[128,16,256]{0,2,1:T(8,128)(2,1)S(1)} %bitcast.334), kind=kLoop, calls=%fused_computation.107 | loop fusion | bytes 311296 | tf_op jit(solution)/shard_map/split | solution.py:81
  57.5 12.5 %slice_reduce_fusion.57 = (bf16[16,256]{1,0:T(8,128)(2,1)S(1)}, bf16[16,256]{1,0:T(8,128)(2,1)S(1)}, bf16[16,256]{1,0:T(8,128)(2,1)S(1)}, bf16[16,256]{1,0:T(8,1...) fusion(bf16[128,16,256]{0,2,1:T(8,128)(2,1)S(1)} %bitcast.335), kind=kLoop, calls=%fused_computation.88 | loop fusion | bytes 311296 | tf_op jit(solution)/shard_map/split | solution.py:81
  70.0 12.4 %slice_reduce_fusion.38 = (bf16[16,256]{1,0:T(8,128)(2,1)S(1)}, bf16[16,256]{1,0:T(8,128)(2,1)S(1)}, bf16[16,256]{1,0:T(8,128)(2,1)S(1)}, bf16[16,256]{1,0:T(8,1...) fusion(bf16[128,16,256]{0,2,1:T(8,128)(2,1)S(1)} %bitcast.336), kind=kLoop, calls=%fused_computation.69 | loop fusion | bytes 311296 | tf_op jit(solution)/shard_map/split | solution.py:81
  82.4 12.4 %slice_reduce_fusion.19 = (bf16[16,256]{1,0:T(8,128)(2,1)S(1)}, bf16[16,256]{1,0:T(8,128)(2,1)S(1)}, bf16[16,256]{1,0:T(8,128)(2,1)S(1)}, bf16[16,256]{1,0:T(8,1...) fusion(bf16[128,16,256]{0,2,1:T(8,128)(2,1)S(1)} %bitcast.337), kind=kLoop, calls=%fused_computation.50 | loop fusion | bytes 311296 | tf_op jit(solution)/shard_map/split | solution.py:81
  94.8 12.6 %slice_reduce_fusion = (bf16[16,256]{1,0:T(8,128)(2,1)S(1)}, bf16[16,256]{1,0:T(8,128)(2,1)S(1)}, bf16[16,256]{1,0:T(8,128)(2,1)S(1)}, bf16[16,256]{1,0:T(8,128)...) fusion(bf16[128,16,256]{0,2,1:T(8,128)(2,1)S(1)} %bitcast.338), kind=kLoop, calls=%fused_computation.31 | loop fusion | bytes 311296 | tf_op jit(solution)/shard_map/split | solution.py:81
  183.5 14.3 %all-to-all-start = ((bf16[128,1,16,256]{3,2,1,0:T(8,128)(2,1)}), bf16[128,1,16,256]{3,2,1,0:T(8,128)(2,1)S(1)}, u32[]{:S(2)}, u32[]{:S(2)}) async-start(bf16[128,1,16,256]{3,2,1,0:T(8,128)(2,1)} %constant_dynamic-update-slice_fusion), calls=%async_computation | async-start | bytes 2097152 | tf_op jit(solution)/shard_map/all_to_all | solution.py:80
  199.5 52.1 %all-to-all-done = bf16[128,1,16,256]{3,2,1,0:T(8,128)(2,1)S(1)} async-done(((bf16[128,1,16,256]{3,2,1,0:T(8,128)(2,1)}), bf16[128,1,16,256]{3,2,1,0:T(8,128)(2,1)S(1)}, u32[]{:S(2)}, u32[]{:S(2)}) %all-to-all-start) | async-done | bytes 1048608 | tf_op jit(solution)/shard_map/all_to_all | solution.py:80
  251.9 1.5 fusion.31
  254.2 37.6 %while.17 = (s32[]{:T(128)}, f32[1,1024]{1,0:T(1,128)S(1)}, f32[1,1024]{1,0:T(1,128)S(1)}, f32[1,1024,128]{2,1,0:T(8,128)S(1)}, s32[17]{0:T(128)S(1)}, /*index=5...) while((s32[]{:T(128)}, f32[1,1024]{1,0:T(1,128)S(1)}, ...), condition=%wide.region_4.5_spmd.clone, body=%wide.region_1.4_spmd.clone.sunk | while | flops 68562176 | bytes 3024009 | solution.py:135
  254.3 0.7 dynamic_slice.38
  254.9 0.7 add_add_fusion.2
  256.5 0.7 dynamic_slice.38
  257.1 0.7 add_add_fusion.2
  258.7 0.7 dynamic_slice.38
  259.4 0.7 add_add_fusion.2
  260.9 0.7 dynamic_slice.38
  261.6 0.7 add_add_fusion.2
  263.1 0.7 dynamic_slice.38
  263.8 0.7 add_add_fusion.2
  265.3 0.7 dynamic_slice.38
  266.0 0.7 add_add_fusion.2
  267.5 0.7 dynamic_slice.38
  268.2 0.7 add_add_fusion.2
  269.8 0.7 dynamic_slice.38
  270.4 0.7 add_add_fusion.2
  272.6 0.7 add_add_fusion.2
  274.2 0.7 dynamic_slice.38
  274.9 0.7 add_add_fusion.2
  276.4 0.7 dynamic_slice.38
  277.1 0.7 add_add_fusion.2
  278.6 0.7 dynamic_slice.38
  279.3 0.7 add_add_fusion.2
  280.8 0.7 dynamic_slice.38
  281.5 0.7 add_add_fusion.2
  283.0 0.7 dynamic_slice.38
  283.7 0.7 add_add_fusion.2
  285.9 0.7 add_add_fusion.2
  287.5 0.7 dynamic_slice.38
  288.1 0.7 add_add_fusion.2
  289.7 0.7 dynamic_slice.38
  290.4 0.7 add_add_fusion.2
  292.1 0.9 select_convert_fusion
  (288 shorter events, 94.3 us)
Async XLA Ops:
  183.5 14.4 %copy-start.2 = (bf16[1,128,128]{2,1,0:T(8,128)(2,1)S(1)}, bf16[1,128,128]{2,1,0:T(8,128)(2,1)}, u32[]{:S(2)}) copy-start(bf16[1,128,128]{2,1,0:T(8,128)(2,1)} %param.11) | copy-start | bytes 98308
  183.5 14.9 %copy-start = (bf16[8,128,128]{2,1,0:T(8,128)(2,1)S(1)}, bf16[8,128,128]{2,1,0:T(8,128)(2,1)}, u32[]{:S(2)}) copy-start(bf16[8,128,128]{2,1,0:T(8,128)(2,1)} %param.10) | copy-start | bytes 786436
  183.5 68.1 %all-to-all-start = ((bf16[128,1,16,256]{3,2,1,0:T(8,128)(2,1)}), bf16[128,1,16,256]{3,2,1,0:T(8,128)(2,1)S(1)}, u32[]{:S(2)}, u32[]{:S(2)}) async-start(bf16[128,1,16,256]{3,2,1,0:T(8,128)(2,1)} %constant_dynamic-update-slice_fusion), calls=%async_computation | async-start | bytes 2097152 | tf_op jit(solution)/shard_map/all_to_all | solution.py:80
  197.8 0.7 copy-start.3
  253.4 0.8 copy-start.1
